TPU v7x, 512 devices: a whole 4x4x16 slice. The times are simulated.
512 devices in a mesh: batch: 16 (over z_hi, y, core), tensor: 32 (over x, z_lo).
Axes of the slice: x: 4, y: 4, z: 16 (z_hi: 2, z_lo: 8; z = z_hi * 8 + z_lo), core: 2. Of those that a mesh axis runs over, the one named last changes fastest.
Arguments:
- tokens: bfloat16 [4096, 4096], P('batch', 'tensor'), may hold values from -6 to 6
- gate_pre: bfloat16 [4096, 14336], P('batch', 'tensor'), may hold values from -8 to 8
- up_pre: bfloat16 [4096, 14336], P('batch', 'tensor'), may hold values from -6 to 6
- down_weight: bfloat16 [14336, 4096], P('tensor'), may hold values from -0.046875 to 0.046875
- tangent_gate: bfloat16 [4096, 14336], P('batch', 'tensor'), may hold values from -0.09375 to 0.09375
- loss_weight: float32 [4096], P('batch'), may hold values from 0.05 to 0.5
Outputs:
- gnvp: float32 [4096, 14336], P('batch', 'tensor')
All inputs are finite; a program needn't handle non-finite values.
Results may differ from a plain program's by a relative error of at most 0.025.
Values may be sent and summed in bfloat16 or wider, within the bound.
A program may use at most 64 MiB of HBM per device.

v0:
```python
import jax
import jax.numpy as jnp
from jax import lax
from jax.sharding import PartitionSpec as P


def slope_of(gate_pre, up_pre):
    a = gate_pre.astype(jnp.float32)
    sig = jax.nn.sigmoid(a)
    return sig * (1.0 + a * (1.0 - sig)) * up_pre.astype(jnp.float32)


def body(tokens, gate_pre, up_pre, down_weight, tangent_gate, loss_weight):
    whole = lax.all_gather(tokens, "tensor", axis=1, tiled=True)
    slope = slope_of(gate_pre, up_pre)
    columns = whole
    tangent_gate_out = jnp.dot(
        columns,
        lax.all_gather(tangent_gate, "batch", axis=0, tiled=True),
        preferred_element_type=jnp.float32,
    )
    tangent_hidden = (slope * tangent_gate_out).astype(jnp.bfloat16)
    partial_out = jnp.dot(tangent_hidden, down_weight, preferred_element_type=jnp.float32)
    tangent_out = lax.psum(partial_out.astype(jnp.bfloat16), "tensor").astype(jnp.float32)
    weighted = (loss_weight[:, None] * tangent_out).astype(jnp.bfloat16)
    back_hidden = jnp.einsum("td,fd->tf", weighted, down_weight, preferred_element_type=jnp.float32)
    back_gate = (back_hidden * slope).astype(jnp.bfloat16)
    columns = whole
    return lax.psum_scatter(
        jnp.einsum("td,tf->df", columns, back_gate, preferred_element_type=jnp.float32).astype(
            jnp.bfloat16
        ),
        "batch",
        scatter_dimension=0,
        tiled=True,
    ).astype(jnp.float32)


def solution(mesh):
    placed = (
        P("batch", "tensor"),
        P("batch", "tensor"),
        P("batch", "tensor"),
        P("tensor", None),
        P("batch", "tensor"),
        P("batch"),
    )
    return jax.shard_map(
        body, mesh=mesh, in_specs=placed, out_specs=P("batch", "tensor"), check_vma=False
    )
```

profile of v0, /device:TPU:25, one launch (start us, length us, event | category | flops | bytes accessed | tf_op | source)
XLA Modules:
  0.0 938.1 jit_solution(17871154214957523726)
XLA Ops:
  6.5 0.0 all-gather.3.cloned.1.call-start
  6.5 0.7 all-gather.3.cloned.1.call-update
  7.3 0.0 all-gather.5.cloned.1.call-start
  7.3 0.7 all-gather.5.cloned.1.call-update
  8.0 0.0 copy-start.1
  8.0 0.0 copy-start.2
  8.0 0.0 copy-start.3
  8.0 0.0 all-reduce.2.cloned.1.call-start
  8.1 180.7 %all-gather.3.cloned.1.call-done = bf16[256,4096]{1,0:T(8,128)(2,1)} async-done(((bf16[256,128]{1,0:T(8,128)(2,1)}), bf16[256,4096]{1,0:T(8,128)(2,1)}) %all-gather.3.cloned.1.call-update) | async-done | bytes 2097168 | tf_op jit(solution)/shard_map/all_gather | solution.py:14
  188.8 0.0 copy-start
  188.8 122.7 %all-gather.5.cloned.1.call-done = bf16[4096,448]{0,1:T(8,128)(2,1)} async-done(((bf16[256,448]{0,1:T(8,128)(2,1)}), bf16[4096,448]{0,1:T(8,128)(2,1)}) %all-gather.5.cloned.1.call-update) | async-done | bytes 3670032 | tf_op jit(solution)/shard_map/all_gather | solution.py:19
  311.5 9.6 %convolution_convert_fusion.1 = bf16[256,4096]{1,0:T(8,128)(2,1)} fusion(bf16[448,4096]{1,0:T(8,128)(2,1)} %param.9, bf16[256,4096]{1,0:T(8,128)(2,1)} %all-gather.3.cloned.1.call-done, bf16[4096,448]{0,1:T(8,128)(2,1)} %all-gather.5.cloned.1.call-done, bf16[256,448]{0,1:T(8,128)(2,1)} %param.7, bf16[256,448]{0,1:T(8,128)(2,1)} %param.8), kind=kOutput, calls=%fused_computation.2 | convolution fusion | flops 1881473024 | bytes 11993088 | tf_op jit(solution)/shard_map/dot_general | solution.py:23
  321.1 0.0 all-reduce.2.cloned.1.call-update
  321.1 0.0 reduce-scatter.2.cloned.1.call-start
  321.2 437.6 %all-reduce.2.cloned.1.call-done = bf16[256,4096]{1,0:T(8,128)(2,1)} async-done(((bf16[256,4096]{1,0:T(8,128)(2,1)}), bf16[256,4096]{1,0:T(8,128)(2,1)}) %all-reduce.2.cloned.1.call-update) | async-done | bytes 2097168 | tf_op jit(solution)/shard_map/psum | solution.py:24
  758.8 0.0 copy-done.1
  758.8 0.0 copy-done.2
  758.8 0.0 copy-done.3
  758.8 0.0 copy-done
  758.8 8.6 fusion
  767.4 0.0 reduce-scatter.2.cloned.1.call-update
  767.4 162.4 %reduce-scatter.2.cloned.1.call-done = bf16[256,448]{0,1:T(8,128)(2,1)} async-done(((bf16[4096,448]{0,1:T(8,128)(2,1)}), bf16[256,448]{0,1:T(8,128)(2,1)}) %reduce-scatter.2.cloned.1.call-update) | async-done | bytes 229392 | tf_op jit(solution)/shard_map/reduce_scatter | solution.py:29
  929.8 1.7 convert_element_type.39
Async XLA Ops:
  6.5 182.3 %all-gather.3.cloned.1.call-start = ((), (), s32[]{:S(2)}) async-start(), calls=%async_computation.1 | async-start | bytes 2162688 | tf_op jit(solution)/shard_map/all_gather | solution.py:14
  7.3 304.3 %all-gather.5.cloned.1.call-start = ((), (), s32[]{:S(2)}) async-start(), calls=%async_computation.2 | async-start | bytes 3899392 | tf_op jit(solution)/shard_map/all_gather | solution.py:19
  8.0 750.8 %copy-start.1 = (bf16[256,448]{0,1:T(8,128)(2,1)S(1)}, bf16[256,448]{0,1:T(8,128)(2,1)}, u32[]{:S(2)}) copy-start(bf16[256,448]{0,1:T(8,128)(2,1)} %param.7) | copy-start | bytes 688132
  8.0 750.8 %copy-start.2 = (bf16[256,448]{0,1:T(8,128)(2,1)S(1)}, bf16[256,448]{0,1:T(8,128)(2,1)}, u32[]{:S(2)}) copy-start(bf16[256,448]{0,1:T(8,128)(2,1)} %param.8) | copy-start | bytes 688132
  8.0 750.8 %copy-start.3 = (f32[256]{0:T(256)S(1)}, f32[256]{0:T(256)}, u32[]{:S(2)}) copy-start(f32[256]{0:T(256)} %param.11) | copy-start | bytes 3076
  8.0 750.8 %all-reduce.2.cloned.1.call-start = ((), (), s32[]{:S(2)}) async-start(), calls=%async_computation.3 | async-start | bytes 4194304 | tf_op jit(solution)/shard_map/psum | solution.py:24
  188.8 570.0 %copy-start = (bf16[256,4096]{1,0:T(8,128)(2,1)S(1)}, bf16[256,4096]{1,0:T(8,128)(2,1)}, u32[]{:S(2)}) copy-start(bf16[256,4096]{1,0:T(8,128)(2,1)} %all-gather.3.cloned.1.call-done) | copy-start | bytes 6291460
  321.1 608.7 %reduce-scatter.2.cloned.1.call-start = ((), (), s32[]{:S(2)}) async-start(), calls=%async_computation.4 | async-start | bytes 3899392 | tf_op jit(solution)/shard_map/reduce_scatter | solution.py:29
Sparse Core Ops, SparseCore 0:
  9.4 179.4 all-gather.2
  192.0 119.5 all-gather.4
  321.2 437.5 all-reduce.1
  767.5 162.2 reduce-scatter.1
where the time goes:
time: 940 us; the launch traced here: 938 us
  waiting for transfers between devices  905 us (96%)
  matrix products  18.1 us (2%)
  between operations  13.2 us (1%)
    psum x1, waiting for transfers between devices, body(): lax.psum(partial_out.astype(jnp.bfloat16), 'tensor').astype(jnp.float32)  438 us
    all_gather x1, waiting for transfers between devices, body(): whole = lax.all_gather(tokens, 'tensor', axis=1, tiled=True)  181 us
    reduce_scatter x1, waiting for transfers between devices, body(): lax.psum_scatter(jnp.einsum('td,tf->df', columns, back_gate, preferred_el...  162 us
    all_gather x1, waiting for transfers between devices, body(): lax.all_gather(tangent_gate, 'batch', axis=0, tiled=True)  123 us
  transfers between devices with their start and end apart: 4, of which 4 were waited for; matrix products, arithmetic and copies ran while one was open for 0% of the time, Pallas kernels for 0%

commit v1 on v0

v1 whole, which is shorter than its diff:
```python
import jax
import jax.numpy as jnp
from jax import lax
from jax.experimental import pallas as pl
from jax.experimental.pallas import tpu as pltpu
from jax.sharding import PartitionSpec as P

MESH = pl.DeviceIdType.MESH
TOK = 256
D = 4096
F = 448
FM = 384
COL = 128
ROWS = 896
ZCH = 4
CH = ROWS // ZCH


def slope_of(gate_pre, up_pre):
    a = gate_pre.astype(jnp.float32)
    sig = jax.nn.sigmoid(a)
    return sig * (1.0 + a * (1.0 - sig)) * up_pre.astype(jnp.float32)


def dot(a, b):
    return jnp.dot(a, b, preferred_element_type=jnp.float32)


def kernel(
    tok_in, gate_in, up_in, w_hbm, tan_in, lw_in, out_ref,
    tok, tokt, tan, relay_a, w, slope, hidden,
    part, merge, cross, quad, quad_in, pair_out, pair_in,
    wt, sib_out, sib_in, own, y_in, z_out, relay_d, z_in, acc, edges,
    send_sem, recv_sem, local_sem,
):
    b = lax.axis_index("batch")
    t = lax.axis_index("tensor")
    zh, y, c = b // 8, (b // 2) % 4, b % 2
    x, zl = t // 8, t % 8
    jq, jr = zl // 4, zl % 4
    z = zh * 8 + zl
    up = 1 - 2 * c

    def at(zh_=zh, y_=y, c_=c, x_=x, zl_=zl):
        return {"batch": zh_ * 8 + y_ * 2 + c_, "tensor": x_ * 8 + zl_}

    def at_z(z_):
        z_ = (z_ + 16) % 16
        return at(zh_=z_ // 8, zl_=z_ % 8)

    xs = [at(x_=(x + k) % 4) for k in range(4)]
    ys = [at(y_=(y + k) % 4) for k in range(4)]
    qs = [at(zl_=jq * 4 + (jr + k) % 4) for k in range(4)]
    pair = at(zl_=(zl + 4) % 8)
    sib = at(c_=1 - c)
    ahead = at_z(z + 4 * up)

    count = [0]
    sent = []

    def copy(src, dst, dev):
        i = count[0]
        count[0] += 1
        return pltpu.make_async_remote_copy(
            src_ref=src, dst_ref=dst, send_sem=send_sem.at[i], recv_sem=recv_sem.at[i],
            device_id=dev, device_id_type=MESH,
        )

    def send(src, dst, dev):
        cp = copy(src, dst, dev)
        cp.start()
        sent.append(cp)
        return count[0] - 1

    def arrived(dst, i):
        pltpu.make_async_remote_copy(
            src_ref=dst, dst_ref=dst, send_sem=send_sem.at[i], recv_sem=recv_sem.at[i],
            device_id=sib, device_id_type=MESH,
        ).wait_recv()

    w_copy = pltpu.make_async_copy(w_hbm, w, local_sem)
    w_copy.start()

    tcol = pl.multiple_of(t * COL, COL)
    tok[:, pl.ds(tcol, COL)] = tok_in[...]
    for i in range(3):
        tan[b, i * TOK : (i + 1) * TOK, :] = tan_in[:, i * COL : (i + 1) * COL]
    tan[b, 3 * TOK :, :] = jnp.concatenate([tan_in[0:128, FM:F], tan_in[128:256, FM:F]], axis=1)

    barrier = pltpu.get_barrier_semaphore()
    partners = xs[1:] + ys[1:] + qs[1:] + [sib, at_z(z + 4), at_z(z - 4)]
    for dev in partners:
        pl.semaphore_signal(barrier, inc=1, device_id=dev, device_id_type=MESH)
    pl.semaphore_wait(barrier, len(partners))

    class Gather:
        def __init__(self, buf):
            self.buf = buf
            self.x_ids = {}

        def piece(self, zp, xp=None, lo=0, n=TOK):
            col = pl.multiple_of(((x if xp is None else xp) * 8 + zp) * COL, COL)
            return self.buf.at[pl.ds(lo, n), pl.ds(col, COL)]

        def pz(self, h, k):
            return ((jq + h) % 2) * 4 + (jr + 4 - k) % 4

        def along_x(self, h, k):
            ref = self.piece(self.pz(h, k))
            self.x_ids[h, k] = [send(ref, ref, xs[1]), send(ref, ref, xs[3])]

        def start(self):
            ref = self.piece(zl)
            self.pair_id = send(ref, ref, pair)
            self.quad_ids = [[None] + [send(ref, ref, qs[k]) for k in (1, 2, 3)], None]
            self.along_x(0, 0)

        def take_pair(self):
            ref = self.piece(self.pz(1, 0))
            arrived(ref, self.pair_id)
            self.quad_ids[1] = [None] + [send(ref, ref, qs[k]) for k in (1, 2, 3)]
            self.along_x(1, 0)

        def take_quad(self, h, k):
            arrived(self.piece(self.pz(h, k)), self.quad_ids[h][k])
            self.along_x(h, k)

        def forward_x(self, h, k):
            zp = self.pz(h, k)
            left, right = (x + 3) % 4, (x + 1) % 4
            arrived(self.piece(zp, left), self.x_ids[h, k][0])
            lo = self.piece(zp, left, 0, TOK // 2)
            ids = [send(lo, lo, xs[1])]
            arrived(self.piece(zp, right), self.x_ids[h, k][1])
            hi = self.piece(zp, right, TOK // 2, TOK // 2)
            ids.append(send(hi, hi, xs[3]))
            self.x_ids[h, k] += ids

        def finish(self, h, k):
            zp = self.pz(h, k)
            far = (x + 2) % 4
            arrived(self.piece(zp, far, 0, TOK // 2), self.x_ids[h, k][2])
            arrived(self.piece(zp, far, TOK // 2, TOK // 2), self.x_ids[h, k][3])

    order = [(0, 0), (0, 1), (0, 2), (0, 3), (1, 0), (1, 1), (1, 2), (1, 3)]

    def chunk(ref, i, n=1):
        return ref.at[pl.ds(i * CH, n * CH), :]

    other = (1 - zh) * 8 + y * 2 + c
    z_src = (z - 4 * up + 16) % 16
    b_src = (z_src // 8) * 8 + y * 2 + c
    own_block = tan.at[b]
    leg1 = [send(chunk(own_block, i), chunk(relay_a, i), ahead) for i in range(ZCH)]
    g = Gather(tok)
    g.start()
    y_own = [None] + [send(own_block, own_block, ys[k]) for k in (1, 2, 3)]
    sib_ids = {}
    sib_ids[0, 0] = send(own_block, own_block, sib)

    slope[...] = slope_of(gate_in[...], up_in[...])

    g.take_pair()
    leg2 = []

    def pass_on(i):
        arrived(chunk(relay_a, i), leg1[i])
        leg2.append(send(chunk(relay_a, i), chunk(tan.at[b_src], i), ahead))

    pass_on(0)
    for k in (1, 2, 3):
        g.take_quad(0, k)
    pass_on(1)
    g.forward_x(0, 0)
    g.forward_x(1, 0)
    pass_on(2)
    for k in (1, 2, 3):
        g.take_quad(1, k)
        g.forward_x(0, k)
    pass_on(3)
    for k in (1, 2, 3):
        g.forward_x(1, k)

    def tan_slot(hz, k):
        return ((zh + hz) % 2) * 8 + ((y + 4 - k) % 4) * 2 + c

    for k in (1, 2, 3):
        ref = tan.at[tan_slot(0, k)]
        arrived(ref, y_own[k])
        sib_ids[0, k] = send(ref, ref, sib)
    y_other = []
    for half in range(2):
        for i in range(2):
            arrived(chunk(tan.at[other], 2 * half + i), leg2[2 * half + i])
        ref = chunk(tan.at[other], 2 * half, 2)
        y_other.append([None] + [send(ref, ref, ys[k]) for k in (1, 2, 3)])
    sib_ids[1, 0] = send(tan.at[other], tan.at[other], sib)
    for k in (1, 2, 3):
        block = tan.at[tan_slot(1, k)]
        arrived(chunk(block, 0, 2), y_other[0][k])
        arrived(chunk(block, 2, 2), y_other[1][k])
        sib_ids[1, k] = send(block, block, sib)
    for h, k in order:
        g.finish(h, k)
    for hz in range(2):
        for k in range(4):
            arrived(tan.at[((zh + hz) % 2) * 8 + ((y + 4 - k) % 4) * 2 + 1 - c], sib_ids[hz, k])

    acc[...] = jnp.zeros_like(acc)

    @pl.loop(0, 16)
    def _(i):
        cols = tok[:, pl.ds(pl.multiple_of(i * TOK, TOK), TOK)]
        main = jnp.concatenate(
            [tan[i, j * TOK : (j + 1) * TOK, :] for j in range(3)], axis=1
        )
        edge = tan[i, 3 * TOK :, :]
        acc[:, 0:FM] += dot(cols, main)
        acc[:, FM : FM + COL] += dot(cols[:, 0:128], edge)
        acc[:, FM + COL :] += dot(cols[:, 128:256], edge)

    hidden[:, 0:FM] = (slope[:, 0:FM] * acc[:, 0:FM]).astype(jnp.bfloat16)
    hidden[:, FM:F] = (
        slope[:, FM:F] * (acc[:, FM : FM + 64] + acc[:, FM + COL + 64 : FM + 2 * COL])
    ).astype(jnp.bfloat16)

    w_copy.wait()

    def zq(h, k):
        return ((jq + h) % 2) * 4 + (jr + k) % 4

    def p_ref(kx, h, k, lo=0, n=TOK):
        col = pl.multiple_of((((x + kx) % 4) * 8 + zq(h, k)) * COL, COL)
        return part.at[pl.ds(lo, n), pl.ds(col, COL)]

    rs = [(1, 1), (1, 2), (1, 3), (1, 0), (0, 1), (0, 2), (0, 3), (0, 0)]
    half = TOK // 2
    m_ids, c_ids, q_ids = {}, {}, {}
    for h in (1, 0):
        for kx in (2, 1, 3, 0):
            col = pl.multiple_of(((x + kx) % 4) * 1024 + ((jq + h) % 2) * 512, 512)
            part[:, pl.ds(col, 512)] = dot(hidden[...], w[:, pl.ds(col, 512)]).astype(jnp.bfloat16)
            if kx == 2:
                for k in (1, 2, 3, 0):
                    n = rs.index((h, k))
                    m_ids[h, k] = [
                        send(p_ref(2, h, k, 0, half), merge.at[0, n], xs[1]),
                        send(p_ref(2, h, k, half, half), merge.at[1, n], xs[3]),
                    ]

    def merge_x(h, k):
        n = rs.index((h, k))
        c_ids[h, k] = []
        for side, kx in ((0, 1), (1, 3)):
            arrived(merge.at[side, n], m_ids[h, k][side])
            ref = p_ref(kx, h, k, side * half, half)
            ref[...] = (
                ref[...].astype(jnp.float32) + merge[side, n].astype(jnp.float32)
            ).astype(jnp.bfloat16)
            c_ids[h, k].append(send(p_ref(kx, h, k), cross.at[side, n], xs[kx]))

    def reduce_x(h, k):
        n = rs.index((h, k))
        arrived(cross.at[0, n], c_ids[h, k][0])
        arrived(cross.at[1, n], c_ids[h, k][1])
        total = (
            p_ref(0, h, k)[...].astype(jnp.float32)
            + cross[0, n].astype(jnp.float32)
            + cross[1, n].astype(jnp.float32)
        )
        if k == 0:
            return total
        quad[n] = total.astype(jnp.bfloat16)
        q_ids[h, k] = send(quad.at[n], quad_in.at[n], qs[k])

    def reduce_quad(h, total):
        for k in (1, 2, 3):
            n = rs.index((h, k))
            arrived(quad_in.at[n], q_ids[h, k])
            total = total + quad_in[n].astype(jnp.float32)
        return total

    for h, k in rs[:6]:
        merge_x(h, k)
    for h, k in rs[:3]:
        reduce_x(h, k)
    for h, k in rs[6:]:
        merge_x(h, k)
    tot1 = reduce_x(1, 0)
    for h, k in rs[4:5]:
        reduce_x(h, k)
    pair_out[...] = reduce_quad(1, tot1).astype(jnp.bfloat16)
    pair_id = send(pair_out, pair_in, pair)
    for h, k in rs[5:7]:
        reduce_x(h, k)
    tot0 = reduce_x(0, 0)
    tot0 = reduce_quad(0, tot0)
    arrived(pair_in, pair_id)
    weight = jnp.transpose(jnp.broadcast_to(lw_in[...], (COL, TOK)))
    wt[:, pl.ds(tcol, COL)] = (
        weight * (tot0 + pair_in[...].astype(jnp.float32))
    ).astype(jnp.bfloat16)

    g = Gather(wt)
    g.start()

    @pl.loop(0, 16)
    def _(i):
        at_i = pl.ds(pl.multiple_of(i * TOK, TOK), TOK)
        tokt[at_i, :] = jnp.transpose(tok[:, at_i])

    g.take_pair()
    for k in (1, 2, 3):
        g.take_quad(0, k)
    g.forward_x(0, 0)
    g.forward_x(1, 0)
    for k in (1, 2, 3):
        g.take_quad(1, k)
        g.forward_x(0, k)
    for k in (1, 2, 3):
        g.forward_x(1, k)
    for h, k in order:
        g.finish(h, k)

    acc[:, 0:F] = jnp.zeros((TOK, F), jnp.float32)

    @pl.loop(0, 8)
    def _(i):
        at_i = pl.ds(pl.multiple_of(i * 512, 512), 512)
        acc[:, 0:F] += lax.dot_general(
            wt[:, at_i], w[:, at_i], (((1,), (1,)), ((), ())), preferred_element_type=jnp.float32
        )

    hidden[...] = (acc[:, 0:F] * slope[...]).astype(jnp.bfloat16)

    back = hidden[...]
    main = back[:, 0:FM]
    edge = back[:, FM:F]
    zero = jnp.zeros_like(edge)
    edges[:, 0:64] = edge
    edges[:, 64:128] = zero
    edges[:, 128:192] = zero
    edges[:, 192:256] = edge
    edge_lo, edge_hi = edges[:, 0:128], edges[:, 128:256]

    def product(blk, emit):
        row = pl.multiple_of(blk * TOK, TOK)
        top = dot(tokt[pl.ds(row, TOK), :], main)
        for j in range(3):
            emit(j * TOK, TOK, top[:, j * COL : (j + 1) * COL])
        low = dot(tokt[pl.ds(row, 128), :], edge_lo) + dot(tokt[pl.ds(row + 128, 128), :], edge_hi)
        emit(3 * TOK, 128, low)

    blocks = [(hz, ky) for hz in (1, 0) for ky in (2, 1, 3, 0)]
    s_ids, y_ids = {}, {}
    for n, (hz, ky) in enumerate(blocks):
        blk = ((zh + hz) % 2) * 8 + ((y + ky) % 4) * 2 + 1 - c

        def emit(lo, rows, val):
            sib_out[n, lo : lo + rows, :] = val.astype(jnp.bfloat16)

        product(blk, emit)
        s_ids[hz, ky] = send(sib_out.at[n], sib_in.at[n], sib)
    for n, (hz, ky) in enumerate(blocks):
        blk = ((zh + hz) % 2) * 8 + ((y + ky) % 4) * 2 + c
        arrived(sib_in.at[n], s_ids[hz, ky])

        def emit(lo, rows, val):
            own[n, lo : lo + rows, :] = (
                val + sib_in[n, lo : lo + rows, :].astype(jnp.float32)
            ).astype(jnp.bfloat16)

        product(blk, emit)
        if ky:
            parts = ZCH if hz else 1
            y_ids[hz, ky] = [
                send(chunk(own.at[n], i, ZCH // parts), chunk(y_in.at[n], i, ZCH // parts), ys[ky])
                for i in range(parts)
            ]

    def rows_of(ref, n, lo, rows):
        return ref[n, lo : lo + rows, :].astype(jnp.float32)

    leg1, leg2 = [], []
    for i in range(ZCH):
        lo = i * CH
        total = rows_of(own, 3, lo, CH)
        for n in range(3):
            arrived(chunk(y_in.at[n], i), y_ids[blocks[n]][i])
            total = total + rows_of(y_in, n, lo, CH)
        z_out[lo : lo + CH, :] = total.astype(jnp.bfloat16)
        leg1.append(send(chunk(z_out, i), chunk(relay_d, i), ahead))
    for i in range(ZCH):
        arrived(chunk(relay_d, i), leg1[i])
        leg2.append(send(chunk(relay_d, i), chunk(z_in, i), ahead))
    for n in range(4, 7):
        arrived(y_in.at[n], y_ids[blocks[n]][0])
    for i in range(ZCH):
        arrived(chunk(z_in, i), leg2[i])

    def final(lo, rows):
        total = rows_of(own, 7, lo, rows) + z_in[lo : lo + rows, :].astype(jnp.float32)
        for n in range(4, 7):
            total = total + rows_of(y_in, n, lo, rows)
        return total

    for j in range(3):
        out_ref[:, j * COL : (j + 1) * COL] = final(j * TOK, TOK)
    low = final(3 * TOK, 128)
    out_ref[0:128, FM:F] = low[:, 0:64]
    out_ref[128:256, FM:F] = low[:, 64:128]

    for cp in sent:
        cp.wait_send()


N_SEM = 192


def body(tokens, gate_pre, up_pre, down_weight, tangent_gate, loss_weight):
    vmem = pl.BlockSpec(memory_space=pltpu.VMEM)
    bf = jnp.bfloat16
    return pl.pallas_call(
        kernel,
        out_shape=jax.ShapeDtypeStruct((TOK, F), jnp.float32),
        in_specs=[vmem, vmem, vmem, pl.BlockSpec(memory_space=pl.ANY), vmem, vmem],
        out_specs=vmem,
        scratch_shapes=[
            pltpu.VMEM((TOK, D), bf),
            pltpu.VMEM((D, TOK), bf),
            pltpu.VMEM((16, ROWS, COL), bf),
            pltpu.VMEM((ROWS, COL), bf),
            pltpu.VMEM((F, D), bf),
            pltpu.VMEM((TOK, F), jnp.float32),
            pltpu.VMEM((TOK, F), bf),
            pltpu.VMEM((TOK, D), bf),
            pltpu.VMEM((2, 8, TOK // 2, COL), bf),
            pltpu.VMEM((2, 8, TOK, COL), bf),
            pltpu.VMEM((8, TOK, COL), bf),
            pltpu.VMEM((8, TOK, COL), bf),
            pltpu.VMEM((TOK, COL), bf),
            pltpu.VMEM((TOK, COL), bf),
            pltpu.VMEM((TOK, D), bf),
            pltpu.VMEM((8, ROWS, COL), bf),
            pltpu.VMEM((8, ROWS, COL), bf),
            pltpu.VMEM((8, ROWS, COL), bf),
            pltpu.VMEM((8, ROWS, COL), bf),
            pltpu.VMEM((ROWS, COL), bf),
            pltpu.VMEM((ROWS, COL), bf),
            pltpu.VMEM((ROWS, COL), bf),
            pltpu.VMEM((TOK, FM + 2 * COL), jnp.float32),
            pltpu.VMEM((TOK, 2 * COL), bf),
            pltpu.SemaphoreType.DMA((N_SEM,)),
            pltpu.SemaphoreType.DMA((N_SEM,)),
            pltpu.SemaphoreType.DMA,
        ],
        compiler_params=pltpu.CompilerParams(
            collective_id=0, has_side_effects=True, vmem_limit_bytes=56 * 2**20
        ),
    )(tokens, gate_pre, up_pre, down_weight, tangent_gate, loss_weight.reshape(1, TOK))


def solution(mesh):
    placed = (
        P("batch", "tensor"),
        P("batch", "tensor"),
        P("batch", "tensor"),
        P("tensor", None),
        P("batch", "tensor"),
        P("batch"),
    )
    return jax.shard_map(
        body, mesh=mesh, in_specs=placed, out_specs=P("batch", "tensor"), check_vma=False
    )
```

time: 940 us -> 173 us (0.18)
  the two profiles are of different devices: /device:TPU:25 before, /device:TPU:12 now
where the time goes in v1:
time: 173 us
  Pallas kernels  165 us (95%)
  local copies, waits for them, and re-layouts  7.34 us (4%)
    pallas_call x1, Pallas kernels, body(): pl.pallas_call(kernel, out_shape=jax.ShapeDtypeStruct((TOK, F), jnp.float...  165 us
    unnamed x3, local copies, waits for them, and re-layouts  5.35 us

profile of v1, /device:TPU:12, one launch (start us, length us, event | category | flops | bytes accessed | tf_op | source)
XLA Modules:
  0.0 172.7 jit_solution(15997059676697549780)
XLA Ops:
  0.0 1.8 %copy.7.gate_in = bf16[256,448]{1,0:T(8,128)(2,1)} copy(bf16[256,448]{0,1:T(8,128)(2,1)} %param.7) | data formatting | bytes 458752 | tf_op args[1]
  1.8 1.8 %copy.8.up_in = bf16[256,448]{1,0:T(8,128)(2,1)} copy(bf16[256,448]{0,1:T(8,128)(2,1)} %param.8) | data formatting | bytes 458752 | tf_op args[2]
  3.6 1.8 %copy.9.tan_in = bf16[256,448]{1,0:T(8,128)(2,1)} copy(bf16[256,448]{0,1:T(8,128)(2,1)} %param.10) | data formatting | bytes 458752 | tf_op args[4]
  5.3 165.4 %shard_map.64 = f32[256,448]{1,0:T(8,128)} custom-call(bf16[256,128]{1,0:T(8,128)(2,1)} %tok_in.1, bf16[256,448]{1,0:T(8,128)(2,1)} %copy.7.gate_in, bf16[256,448]{1,0:T(8,128)(2,1)} %copy.8.up_in, bf16[448,4096]{1,0:T(8,128)(2,1)} %w_hbm.1, bf16[256,448]{1,0:T(8,128)(2,1)} %copy.9.tan_in, f32[1,256]{1,0:T(1,128)} %bitcast.1), custom_call_target="tpu_custom_call" | custom-call | tf_op jit(solution)/shard_map/pallas_call | solution.py:423
  170.7 2.0 %copy.10 = f32[256,448]{0,1:T(8,128)} copy(f32[256,448]{1,0:T(8,128)} %shard_map.64) | data formatting | bytes 917504 | tf_op jit(solution)/shard_map/pallas_call | solution.py:423

commit v2 on v1

v2 whole, which is shorter than its diff:
```python
import jax
import jax.numpy as jnp
from jax import lax
from jax.experimental import pallas as pl
from jax.experimental.pallas import tpu as pltpu
from jax.sharding import PartitionSpec as P

MESH = pl.DeviceIdType.MESH
TOK = 256
D = 4096
F = 448
COL = 128
ZCH = 4
CH = F // ZCH
NT = (((1,), (1,)), ((), ()))


def slope_of(gate_pre, up_pre):
    a = gate_pre.astype(jnp.float32)
    sig = jax.nn.sigmoid(a)
    return sig * (1.0 + a * (1.0 - sig)) * up_pre.astype(jnp.float32)


def dot(a, b):
    return jnp.dot(a, b, preferred_element_type=jnp.float32)


def kernel(
    tok_in, gate_in, up_in, w_hbm, tan_in, lw_in, out_ref,
    tok, tan, relay_a, w, slope, hidden,
    part, merge, cross, quad, quad_in, pair_out, pair_in,
    wt, tok_sib, back, back_in, own, y_in, z_out, relay_d, z_in, acc,
    send_sem, recv_sem, local_sem,
):
    b = lax.axis_index("batch")
    t = lax.axis_index("tensor")
    zh, y, c = b // 8, (b // 2) % 4, b % 2
    x, zl = t // 8, t % 8
    jq, jr = zl // 4, zl % 4
    z = zh * 8 + zl
    up = 1 - 2 * c

    def at(zh_=zh, y_=y, c_=c, x_=x, zl_=zl):
        return {"batch": zh_ * 8 + y_ * 2 + c_, "tensor": x_ * 8 + zl_}

    def at_z(z_):
        z_ = (z_ + 16) % 16
        return at(zh_=z_ // 8, zl_=z_ % 8)

    xs = [at(x_=(x + k) % 4) for k in range(4)]
    ys = [at(y_=(y + k) % 4) for k in range(4)]
    qs = [at(zl_=jq * 4 + (jr + k) % 4) for k in range(4)]
    pair = at(zl_=(zl + 4) % 8)
    sib = at(c_=1 - c)
    ahead = at_z(z + 4 * up)

    count = [0]
    sent = []

    def copy(src, dst, dev):
        i = count[0]
        count[0] += 1
        return pltpu.make_async_remote_copy(
            src_ref=src, dst_ref=dst, send_sem=send_sem.at[i], recv_sem=recv_sem.at[i],
            device_id=dev, device_id_type=MESH,
        )

    def send(src, dst, dev):
        cp = copy(src, dst, dev)
        cp.start()
        sent.append(cp)
        return count[0] - 1

    def arrived(dst, i):
        pltpu.make_async_remote_copy(
            src_ref=dst, dst_ref=dst, send_sem=send_sem.at[i], recv_sem=recv_sem.at[i],
            device_id=sib, device_id_type=MESH,
        ).wait_recv()

    w_copy = pltpu.make_async_copy(w_hbm, w, local_sem)
    w_copy.start()

    tcol = pl.multiple_of(t * COL, COL)
    tok[:, pl.ds(tcol, COL)] = tok_in[...]
    tan[b] = tan_in[...]

    barrier = pltpu.get_barrier_semaphore()
    partners = xs[1:] + ys[1:] + qs[1:] + [sib, at_z(z + 4), at_z(z - 4)]
    for dev in partners:
        pl.semaphore_signal(barrier, inc=1, device_id=dev, device_id_type=MESH)
    pl.semaphore_wait(barrier, len(partners))

    class Gather:
        def __init__(self, buf):
            self.buf = buf
            self.x_ids = {}

        def piece(self, zp, xp=None, lo=0, n=TOK):
            col = pl.multiple_of(((x if xp is None else xp) * 8 + zp) * COL, COL)
            return self.buf.at[pl.ds(lo, n), pl.ds(col, COL)]

        def pz(self, h, k):
            return ((jq + h) % 2) * 4 + (jr + 4 - k) % 4

        def along_x(self, h, k):
            ref = self.piece(self.pz(h, k))
            self.x_ids[h, k] = [send(ref, ref, xs[1]), send(ref, ref, xs[3])]

        def start(self):
            ref = self.piece(zl)
            self.pair_id = send(ref, ref, pair)
            self.quad_ids = [[None] + [send(ref, ref, qs[k]) for k in (1, 2, 3)], None]
            self.along_x(0, 0)

        def take_pair(self):
            ref = self.piece(self.pz(1, 0))
            arrived(ref, self.pair_id)
            self.quad_ids[1] = [None] + [send(ref, ref, qs[k]) for k in (1, 2, 3)]
            self.along_x(1, 0)

        def take_quad(self, h, k):
            arrived(self.piece(self.pz(h, k)), self.quad_ids[h][k])
            self.along_x(h, k)

        def forward_x(self, h, k):
            zp = self.pz(h, k)
            left, right = (x + 3) % 4, (x + 1) % 4
            arrived(self.piece(zp, left), self.x_ids[h, k][0])
            lo = self.piece(zp, left, 0, TOK // 2)
            ids = [send(lo, lo, xs[1])]
            arrived(self.piece(zp, right), self.x_ids[h, k][1])
            hi = self.piece(zp, right, TOK // 2, TOK // 2)
            ids.append(send(hi, hi, xs[3]))
            self.x_ids[h, k] += ids

        def finish(self, h, k):
            zp = self.pz(h, k)
            far = (x + 2) % 4
            arrived(self.piece(zp, far, 0, TOK // 2), self.x_ids[h, k][2])
            arrived(self.piece(zp, far, TOK // 2, TOK // 2), self.x_ids[h, k][3])

    order = [(0, 0), (0, 1), (0, 2), (0, 3), (1, 0), (1, 1), (1, 2), (1, 3)]

    def chunk(ref, i, n=1):
        return ref.at[pl.ds(i * CH, n * CH), :]

    other = (1 - zh) * 8 + y * 2 + c
    z_src = (z - 4 * up + 16) % 16
    b_src = (z_src // 8) * 8 + y * 2 + c
    own_block = tan.at[b]
    leg1 = [send(chunk(own_block, i), chunk(relay_a, i), ahead) for i in range(ZCH)]
    g = Gather(tok)
    g.start()
    sib_own = [send(own_block, own_block, sib), None, None, None]

    slope[...] = slope_of(gate_in[...], up_in[...])

    def tan_slot(hz, k, c_=c):
        return ((zh + hz) % 2) * 8 + ((y + 4 - k) % 4) * 2 + c_

    leg2, y_other, sib_other = [], [], [[None] * ZCH for _ in range(4)]

    def pass_on(i):
        arrived(chunk(relay_a, i), leg1[i])
        leg2.append(send(chunk(relay_a, i), chunk(tan.at[b_src], i), ahead))

    def spread(i):
        ref = chunk(tan.at[other], i)
        arrived(ref, leg2[i])
        y_other.append([None] + [send(ref, ref, ys[k]) for k in (1, 2, 3)])
        sib_other[0][i] = send(ref, ref, sib)

    def share_own(k):
        ref = tan.at[tan_slot(0, k)]
        arrived(ref, y_own[k])
        sib_own[k] = send(ref, ref, sib)

    def share_other(k, i):
        ref = chunk(tan.at[tan_slot(1, k)], i)
        arrived(ref, y_other[i][k])
        sib_other[k][i] = send(ref, ref, sib)

    g.take_pair()
    pass_on(0)
    y_own = [None] + [send(own_block, own_block, ys[k]) for k in (1, 2, 3)]
    for k in (1, 2, 3):
        g.take_quad(0, k)
        pass_on(k)
    for k in (1, 3, 2):
        share_own(k)
    for k in (1, 2, 3):
        g.take_quad(1, k)
    spread(0)
    g.forward_x(0, 0)
    g.forward_x(1, 0)
    spread(1)
    for k in (1, 2, 3):
        g.forward_x(0, k)
    spread(2)
    for k in (1, 2, 3):
        g.forward_x(1, k)
    spread(3)
    for i in range(ZCH):
        for k in (1, 3, 2):
            share_other(k, i)
    for h, k in order:
        g.finish(h, k)
    for k in range(4):
        arrived(tan.at[tan_slot(0, k, 1 - c)], sib_own[k])

    def tangent_part(first):
        lhs = jnp.concatenate([tan[first + j] for j in range(4)], axis=1)
        rhs = tok[:, pl.ds(pl.multiple_of(first * TOK, 4 * TOK), 4 * TOK)]
        return lax.dot_general(lhs, rhs, NT, preferred_element_type=jnp.float32)

    acc[...] = tangent_part(zh * 8)
    acc[...] += tangent_part(zh * 8 + 4)
    for k in range(4):
        for i in range(ZCH):
            arrived(chunk(tan.at[tan_slot(1, k, 1 - c)], i), sib_other[k][i])
    acc[...] += tangent_part((1 - zh) * 8)
    tgo = acc[...] + tangent_part((1 - zh) * 8 + 4)
    hidden[...] = jnp.transpose((slope[...] * tgo).astype(jnp.bfloat16))

    tok_id = send(tok, tok_sib, sib)
    w_copy.wait()

    def zq(h, k):
        return ((jq + h) % 2) * 4 + (jr + k) % 4

    def p_ref(kx, h, k, lo=0, n=TOK):
        col = pl.multiple_of((((x + kx) % 4) * 8 + zq(h, k)) * COL, COL)
        return part.at[pl.ds(lo, n), pl.ds(col, COL)]

    rs = [(1, 1), (1, 2), (1, 3), (1, 0), (0, 1), (0, 2), (0, 3), (0, 0)]
    half = TOK // 2
    m_ids, c_ids, q_ids = {}, {}, {}
    for h in (1, 0):
        for kx in (2, 1, 3, 0):
            col = pl.multiple_of(((x + kx) % 4) * 1024 + ((jq + h) % 2) * 512, 512)
            part[:, pl.ds(col, 512)] = dot(hidden[...], w[:, pl.ds(col, 512)]).astype(jnp.bfloat16)
            if kx == 2:
                for k in (1, 2, 3, 0):
                    n = rs.index((h, k))
                    m_ids[h, k] = [
                        send(p_ref(2, h, k, 0, half), merge.at[0, n], xs[1]),
                        send(p_ref(2, h, k, half, half), merge.at[1, n], xs[3]),
                    ]

    def merge_x(h, k):
        n = rs.index((h, k))
        c_ids[h, k] = []
        for side, kx in ((0, 1), (1, 3)):
            arrived(merge.at[side, n], m_ids[h, k][side])
            ref = p_ref(kx, h, k, side * half, half)
            ref[...] = (
                ref[...].astype(jnp.float32) + merge[side, n].astype(jnp.float32)
            ).astype(jnp.bfloat16)
            c_ids[h, k].append(send(p_ref(kx, h, k), cross.at[side, n], xs[kx]))

    def reduce_x(h, k):
        n = rs.index((h, k))
        arrived(cross.at[0, n], c_ids[h, k][0])
        arrived(cross.at[1, n], c_ids[h, k][1])
        total = (
            p_ref(0, h, k)[...].astype(jnp.float32)
            + cross[0, n].astype(jnp.float32)
            + cross[1, n].astype(jnp.float32)
        )
        if k == 0:
            return total
        quad[n] = total.astype(jnp.bfloat16)
        q_ids[h, k] = send(quad.at[n], quad_in.at[n], qs[k])

    def reduce_quad(h, total):
        for k in (1, 2, 3):
            n = rs.index((h, k))
            arrived(quad_in.at[n], q_ids[h, k])
            total = total + quad_in[n].astype(jnp.float32)
        return total

    for h, k in rs[:4]:
        merge_x(h, k)
    for h, k in rs[:3]:
        reduce_x(h, k)
    tot1 = reduce_x(1, 0)
    for h, k in rs[4:]:
        merge_x(h, k)
    pair_out[...] = reduce_quad(1, tot1).astype(jnp.bfloat16)
    pair_id = send(pair_out, pair_in, pair)
    for h, k in rs[4:7]:
        reduce_x(h, k)
    tot0 = reduce_x(0, 0)
    tot0 = reduce_quad(0, tot0)
    arrived(pair_in, pair_id)
    weight = jnp.transpose(jnp.broadcast_to(lw_in[...], (COL, TOK)))
    wt[:, pl.ds(tcol, COL)] = (
        weight * (tot0 + pair_in[...].astype(jnp.float32))
    ).astype(jnp.bfloat16)

    g = Gather(wt)
    g.start()

    def back_part(xp):
        cols = pl.ds(pl.multiple_of(xp * 1024, 1024), 1024)
        return lax.dot_general(w[:, cols], wt[:, cols], NT, preferred_element_type=jnp.float32)

    g.take_pair()
    for k in (1, 2, 3):
        g.take_quad(0, k)
    for k in (1, 2, 3):
        g.take_quad(1, k)
    g.forward_x(0, 0)
    g.forward_x(1, 0)
    acc[...] = back_part(x)
    for k in (1, 2, 3):
        g.forward_x(0, k)
    for k in (1, 2, 3):
        g.forward_x(1, k)
    acc[...] += back_part((x + 1) % 4)
    acc[...] += back_part((x + 3) % 4)
    for h, k in order:
        g.finish(h, k)

    back_hidden = acc[...] + back_part((x + 2) % 4)
    back[...] = (back_hidden * slope[...]).astype(jnp.bfloat16)

    back_id = send(back, back_in, sib)
    arrived(tok_sib, tok_id)
    arrived(back_in, back_id)
    y_ids = {}

    def to_y(hz):
        for i in (0, 2):
            rows = slice(i * CH, (i + 2) * CH)
            lhs = jnp.concatenate([back[rows, :], back_in[rows, :]], axis=1)
            for ky in (2, 1, 3, 0):
                blk = ((zh + hz) % 2) * 8 + ((y + ky) % 4) * 2 + c
                cols = pl.ds(pl.multiple_of(blk * TOK, TOK), TOK)
                term = dot(lhs, jnp.concatenate([tok[:, cols], tok_sib[:, cols]], axis=0))
                for j in (0, 1):
                    own[hz, i + j, ky] = term[j * CH : (j + 1) * CH].astype(jnp.bfloat16)
                    if ky:
                        ref = own.at[hz, i + j, ky]
                        y_ids[hz, ky, i + j] = send(ref, y_in.at[hz, i + j, ky], ys[ky])

    def y_sum(hz, i):
        total = own[hz, i, 0].astype(jnp.float32)
        for ky in (1, 3, 2):
            arrived(y_in.at[hz, i, ky], y_ids[hz, ky, i])
            total = total + y_in[hz, i, ky].astype(jnp.float32)
        return total

    chunks = range(ZCH)
    to_y(1)
    leg1, leg2 = [], []
    for i in chunks:
        z_out[i * CH : (i + 1) * CH, :] = y_sum(1, i).astype(jnp.bfloat16)
        leg1.append(send(chunk(z_out, i), chunk(relay_d, i), ahead))
    to_y(0)
    for i in chunks:
        arrived(chunk(relay_d, i), leg1[i])
        leg2.append(send(chunk(relay_d, i), chunk(z_in, i), ahead))
    for i in chunks:
        out_ref[i * CH : (i + 1) * CH, :] = y_sum(0, i)
    for i in chunks:
        arrived(chunk(z_in, i), leg2[i])
        out_ref[i * CH : (i + 1) * CH, :] += z_in[i * CH : (i + 1) * CH, :].astype(jnp.float32)

    for cp in sent:
        cp.wait_send()


N_SEM = 208


def body(tokens, gate_pre, up_pre, down_weight, tangent_gate, loss_weight):
    vmem = pl.BlockSpec(memory_space=pltpu.VMEM)
    bf = jnp.bfloat16
    return pl.pallas_call(
        kernel,
        out_shape=jax.ShapeDtypeStruct((F, TOK), jnp.float32),
        in_specs=[vmem, vmem, vmem, pl.BlockSpec(memory_space=pl.ANY), vmem, vmem],
        out_specs=vmem,
        scratch_shapes=[
            pltpu.VMEM((TOK, D), bf),
            pltpu.VMEM((16, F, TOK), bf),
            pltpu.VMEM((F, TOK), bf),
            pltpu.VMEM((F, D), bf),
            pltpu.VMEM((F, TOK), jnp.float32),
            pltpu.VMEM((TOK, F), bf),
            pltpu.VMEM((TOK, D), bf),
            pltpu.VMEM((2, 8, TOK // 2, COL), bf),
            pltpu.VMEM((2, 8, TOK, COL), bf),
            pltpu.VMEM((8, TOK, COL), bf),
            pltpu.VMEM((8, TOK, COL), bf),
            pltpu.VMEM((TOK, COL), bf),
            pltpu.VMEM((TOK, COL), bf),
            pltpu.VMEM((TOK, D), bf),
            pltpu.VMEM((TOK, D), bf),
            pltpu.VMEM((F, TOK), bf),
            pltpu.VMEM((F, TOK), bf),
            pltpu.VMEM((2, ZCH, 4, CH, TOK), bf),
            pltpu.VMEM((2, ZCH, 4, CH, TOK), bf),
            pltpu.VMEM((F, TOK), bf),
            pltpu.VMEM((F, TOK), bf),
            pltpu.VMEM((F, TOK), bf),
            pltpu.VMEM((F, TOK), jnp.float32),
            pltpu.SemaphoreType.DMA((N_SEM,)),
            pltpu.SemaphoreType.DMA((N_SEM,)),
            pltpu.SemaphoreType.DMA,
        ],
        compiler_params=pltpu.CompilerParams(
            collective_id=0, has_side_effects=True, vmem_limit_bytes=56 * 2**20
        ),
    )(
        tokens, gate_pre.T, up_pre.T, down_weight, tangent_gate.T, loss_weight.reshape(1, TOK)
    ).T


def solution(mesh):
    placed = (
        P("batch", "tensor"),
        P("batch", "tensor"),
        P("batch", "tensor"),
        P("tensor", None),
        P("batch", "tensor"),
        P("batch"),
    )
    return jax.shard_map(
        body, mesh=mesh, in_specs=placed, out_specs=P("batch", "tensor"), check_vma=False
    )
```

time: 173 us -> 152 us (0.88)
  the two profiles are of different devices: /device:TPU:12 before, /device:TPU:80 now
where the time goes in v2:
time: 152 us
  Pallas kernels  150 us (99%)
  local copies, waits for them, and re-layouts  1.82 us (1%)
    pallas_call x1, Pallas kernels, body(): pl.pallas_call(kernel, out_shape=jax.ShapeDtypeStruct((F, TOK), jnp.float...  150 us

profile of v2, /device:TPU:80, one launch (start us, length us, event | category | flops | bytes accessed | tf_op | source)
XLA Modules:
  0.0 152.0 jit_solution(14600283385898080815)
XLA Ops:
  0.0 150.1 %shard_map.64 = f32[448,256]{1,0:T(8,128)} custom-call(bf16[256,128]{1,0:T(8,128)(2,1)} %tok_in.1, bf16[448,256]{1,0:T(8,128)(2,1)} %bitcast.6, bf16[448,256]{1,0:T(8,128)(2,1)} %bitcast.7, bf16[448,4096]{1,0:T(8,128)(2,1)} %w_hbm.1, bf16[448,256]{1,0:T(8,128)(2,1)} %bitcast.8, f32[1,256]{1,0:T(1,128)} %bitcast.9), custom_call_target="tpu_custom_call" | custom-call | tf_op jit(solution)/shard_map/pallas_call | solution.py:380
  150.1 1.8 %copy.8 = f32[256,448]{0,1:T(8,128)} copy(f32[256,448]{0,1:T(8,128)} %bitcast.5) | data formatting | bytes 917504

commit v3 on v2

--- a/solution.py
+++ b/solution.py
@@ -26,10 +26,10 @@
 
 
 def kernel(
-    tok_in, gate_in, up_in, w_hbm, tan_in, lw_in, out_ref,
+    tok_in, gate_in, up_in, w_hbm, tan_in, lw_in, out_ref, z_in,
     tok, tan, relay_a, w, slope, hidden,
     part, merge, cross, quad, quad_in, pair_out, pair_in,
-    wt, tok_sib, back, back_in, own, y_in, z_out, relay_d, z_in, acc,
+    wt, tok_sib, back, back_in, own, y_in, z_out, relay_d, acc,
     send_sem, recv_sem, local_sem,
 ):
     b = lax.axis_index("batch")
@@ -222,7 +222,15 @@
     tgo = acc[...] + tangent_part((1 - zh) * 8 + 4)
     hidden[...] = jnp.transpose((slope[...] * tgo).astype(jnp.bfloat16))
 
-    tok_id = send(tok, tok_sib, sib)
+    tok_ids = {}
+
+    def tok_block(buf, n, c_):
+        return buf.at[:, pl.ds(pl.multiple_of((2 * n + c_) * TOK, TOK), TOK)]
+
+    def share_tok(first, n):
+        for j in range(first, first + n):
+            tok_ids[j] = send(tok_block(tok, j, 1 - c), tok_block(tok_sib, j, 1 - c), sib)
+
     w_copy.wait()
 
     def zq(h, k):
@@ -317,6 +325,7 @@
         g.forward_x(0, k)
     for k in (1, 2, 3):
         g.forward_x(1, k)
+    share_tok(0, 8)
     acc[...] += back_part((x + 1) % 4)
     acc[...] += back_part((x + 3) % 4)
     for h, k in order:
@@ -326,19 +335,20 @@
     back[...] = (back_hidden * slope[...]).astype(jnp.bfloat16)
 
     back_id = send(back, back_in, sib)
-    arrived(tok_sib, tok_id)
+    for n in range(8):
+        arrived(tok_block(tok_sib, n, c), tok_ids[n])
     arrived(back_in, back_id)
     y_ids = {}
 
     def to_y(hz):
-        for i in (0, 2):
-            rows = slice(i * CH, (i + 2) * CH)
+        for i in range(4):
+            rows = slice(i * CH, (i + 1) * CH)
             lhs = jnp.concatenate([back[rows, :], back_in[rows, :]], axis=1)
             for ky in (2, 1, 3, 0):
                 blk = ((zh + hz) % 2) * 8 + ((y + ky) % 4) * 2 + c
                 cols = pl.ds(pl.multiple_of(blk * TOK, TOK), TOK)
                 term = dot(lhs, jnp.concatenate([tok[:, cols], tok_sib[:, cols]], axis=0))
-                for j in (0, 1):
+                for j in (0,):
                     own[hz, i + j, ky] = term[j * CH : (j + 1) * CH].astype(jnp.bfloat16)
                     if ky:
                         ref = own.at[hz, i + j, ky]
@@ -365,7 +375,6 @@
         out_ref[i * CH : (i + 1) * CH, :] = y_sum(0, i)
     for i in chunks:
         arrived(chunk(z_in, i), leg2[i])
-        out_ref[i * CH : (i + 1) * CH, :] += z_in[i * CH : (i + 1) * CH, :].astype(jnp.float32)
 
     for cp in sent:
         cp.wait_send()
@@ -377,11 +386,14 @@
 def body(tokens, gate_pre, up_pre, down_weight, tangent_gate, loss_weight):
     vmem = pl.BlockSpec(memory_space=pltpu.VMEM)
     bf = jnp.bfloat16
-    return pl.pallas_call(
+    near, far = pl.pallas_call(
         kernel,
-        out_shape=jax.ShapeDtypeStruct((F, TOK), jnp.float32),
+        out_shape=[
+            jax.ShapeDtypeStruct((F, TOK), jnp.float32),
+            jax.ShapeDtypeStruct((F, TOK), bf),
+        ],
         in_specs=[vmem, vmem, vmem, pl.BlockSpec(memory_space=pl.ANY), vmem, vmem],
-        out_specs=vmem,
+        out_specs=[vmem, vmem],
         scratch_shapes=[
             pltpu.VMEM((TOK, D), bf),
             pltpu.VMEM((16, F, TOK), bf),
@@ -404,7 +416,6 @@
             pltpu.VMEM((2, ZCH, 4, CH, TOK), bf),
             pltpu.VMEM((F, TOK), bf),
             pltpu.VMEM((F, TOK), bf),
-            pltpu.VMEM((F, TOK), bf),
             pltpu.VMEM((F, TOK), jnp.float32),
             pltpu.SemaphoreType.DMA((N_SEM,)),
             pltpu.SemaphoreType.DMA((N_SEM,)),
@@ -415,7 +426,8 @@
         ),
     )(
         tokens, gate_pre.T, up_pre.T, down_weight, tangent_gate.T, loss_weight.reshape(1, TOK)
-    ).T
+    )
+    return (near + far.astype(jnp.float32)).T
 
 
 def solution(mesh):

time: 152 us -> 153 us (level)
  the two profiles are of different devices: /device:TPU:80 before, /device:TPU:25 now
where the time goes in v3:
time: 153 us
  Pallas kernels  151 us (99%)
  other arithmetic  1.89 us (1%)
    pallas_call x1, Pallas kernels, body(): pl.pallas_call(kernel, out_shape=[jax.ShapeDtypeStruct((F, TOK), jnp.floa...  151 us

profile of v3, /device:TPU:25, one launch (start us, length us, event | category | flops | bytes accessed | tf_op | source)
XLA Modules:
  0.0 152.5 jit_solution(10470746471569609340)
XLA Ops:
  0.0 150.6 %shard_map.64 = (f32[448,256]{1,0:T(8,128)}, bf16[448,256]{1,0:T(8,128)(2,1)}) custom-call(bf16[256,128]{1,0:T(8,128)(2,1)} %tok_in.1, bf16[448,256]{1,0:T(8,128)(2,1)} %bitcast.6, bf16[448,256]{1,0:T(8,128)(2,1)} %bitcast.7, bf16[448,4096]{1,0:T(8,128)(2,1)} %w_hbm.1, bf16[448,256]{1,0:T(8,128)(2,1)} %bitcast.8, f32[1,256]{1,0:T(1,128)} %bitcast.9), custom_call_target="tpu_custom_call" | custom-call | tf_op jit(solution)/shard_map/pallas_call | solution.py:389
  150.6 1.9 %add_bitcast_fusion = f32[256,448]{0,1:T(8,128)} fusion(f32[448,256]{1,0:T(8,128)} %get-tuple-element.7, bf16[448,256]{1,0:T(8,128)(2,1)} %get-tuple-element.8), kind=kLoop, calls=%fused_computation | loop fusion | flops 229376 | bytes 1146880 | tf_op jit(solution)/shard_map/transpose | solution.py:430
